TPU v7x, 128 devices: a whole 4x4x4 slice. The times are simulated.
128 devices in a mesh: dp: 32 (over z, y, x_hi), expert: 4 (over x_lo, core).
Axes of the slice: x: 4 (x_hi: 2, x_lo: 2; x = x_hi * 2 + x_lo), y: 4, z: 4, core: 2. Of those that a mesh axis runs over, the one named last changes fastest.
Arguments:
- resid: bfloat16 [16384, 2048], P(('dp', 'expert')), may hold values from -6 to 6
- norm_gain: float32 [2048], replicated, may hold values from 0.25 to 1.75
- w_gate: bfloat16 [128, 2048, 768], P(('dp', 'expert')), may hold values from -0.125 to 0.125
- w_up: bfloat16 [128, 2048, 768], P(('dp', 'expert')), may hold values from -0.125 to 0.125
- w_down: bfloat16 [128, 768, 2048], P(('dp', 'expert')), may hold values from -0.21875 to 0.21875
- route_ids: int32 [16384, 8], P(('dp', 'expert')), may hold values from 0 to 127, as said below
- route_slots: int32 [16384, 8], P(('dp', 'expert')), may hold values from -1 to 19, as said below
- route_weights: float32 [16384, 8], P(('dp', 'expert')), may hold values from 0.02 to 0.5
Outputs:
- stream_out: bfloat16 [16384, 2048], P(('dp', 'expert'))
Inputs may be any that keep to these rules, and one draw needn't show every extreme that they name: `route_ids`: each row names 8 different experts. `route_slots`: -1 marks a dropped choice. Among the rows of one device, the kept choices of one expert hold the slots 0, 1, 2, ... without repeats. Three experts, the same for all devices, have slots below 20; all others have slots below 10. On every device each of those three fills all 20 of its slots and some other expert fills all 10.
All inputs are finite; a program needn't handle non-finite values.
Results may differ from a plain program's by a relative error of at most 0.0044.
Values may be sent and summed in bfloat16 or wider, within the bound.
A program may use at most 128 MiB of HBM per device.

v0:
```python
import functools

import jax
import jax.numpy as jnp
from jax import lax
from jax.experimental import pallas as pl
from jax.experimental.pallas import tpu as pltpu
from jax.sharding import PartitionSpec as P

MESH = pl.DeviceIdType.MESH
F32 = jnp.float32
BF16 = jnp.bfloat16
epsilon = 1e-06

TOK = 128
D = 2048
FF = 768
FAN = 8
CAP = 20
MAIN = 24
OVER = 16
WAYS = ((2, 1, 0), (0, 2, 1), (1, 0, 2))
WIDTH = (384, 384, 256)
START = (0, 384, 768)
HALF = 1024


def my_place():
    dp = lax.axis_index("dp")
    ex = lax.axis_index("expert")
    return [(dp % 2) * 2 + ex // 2, (dp // 2) % 4, dp // 8], ex % 2


def device(place, core):
    x, y, z = place
    return (z * 8 + y * 2 + x // 2, (x % 2) * 2 + core)


def moved(place, axis, step):
    place = list(place)
    place[axis] = (place[axis] + step) % 4
    return place


def kernel(main, over, resid, gain, ids, slots, wts, wg_hbm, wu_hbm, wd_hbm, out, *scratch):
    if over:
        flag, *scratch = scratch
    it = iter(scratch)

    def take(n):
        return tuple(next(it) for _ in range(n))

    toks, gs, rs, xs, acc2, acc1 = (take(3) for _ in range(6))
    tab, tab1, tab2s, tab2, hidden, wg, wu, wd = take(8)
    sem_w, s1s, s1r, t1s, t1r, s2s, s2r, t2s, t2r, s3s, s3r, ras, rar, rbs, rbr, rcs, rcr, q2s, q2r, q1s, q1r, free = take(22)
    if over:
        ro, xo, ys = (take(3) for _ in range(3))
        s3os, s3or, fos, fors, oas, oar, obs, obr, ocs, ocr, yss, ysr = take(12)
    main_slots, over_slots = main // 2, over // 2
    ROWS = 8 * main + 4 * over
    LANES = tab.shape[-1]
    place, core = my_place()

    def remote(src, dst, ssem, rsem, where, c):
        return pltpu.make_async_remote_copy(
            src_ref=src, dst_ref=dst, send_sem=ssem, recv_sem=rsem,
            device_id=device(where, c), device_id_type=MESH,
        )

    loads = [pltpu.make_async_copy(h, v, sem_w.at[i]) for i, (h, v) in enumerate(((wg_hbm, wg), (wu_hbm, wu), (wd_hbm, wd)))]
    for cp in loads:
        cp.start()

    barrier = pltpu.get_barrier_semaphore()
    for axis in range(3):
        for step in (1, 2, 3):
            for c in range(2):
                pl.semaphore_signal(barrier, inc=1, device_id=device(moved(place, axis, step), c), device_id_type=MESH)
    pl.semaphore_signal(barrier, inc=1, device_id=device(place, 1 - core), device_id_type=MESH)

    floats = resid[...].astype(F32)
    mean_square = jnp.mean(floats * floats, axis=1, keepdims=True)
    normed = (floats * lax.rsqrt(mean_square + epsilon) * gain[...]).astype(BF16)
    for o in range(3):
        for h in range(2):
            lo = h * HALF + START[o]
            toks[o][h] = normed[:, lo:lo + WIDTH[o]]

    pl.semaphore_wait(barrier, 19)

    def first(o, step, cc):
        one, two, _ = WAYS[o]
        h = (core + cc) % 2
        return remote(
            toks[o].at[h], gs[o].at[place[two], place[one], core],
            s1s.at[o, step, cc], s1r.at[o, step, cc], moved(place, one, step), h,
        )

    for step in (1, 3, 2, 0):
        for o in range(3):
            for cc in range(2):
                if step or cc:
                    first(o, step, cc).start()
    for o in range(3):
        one, two, _ = WAYS[o]
        gs[o][place[two], place[one], core] = toks[o][core]

    e = ids[...]
    coords = ((e >> 1) & 3, (e >> 3) & 3, e >> 5)
    sl = slots[...]
    lane = lax.broadcasted_iota(jnp.int32, (TOK, LANES), 1).astype(F32)
    level = lax.broadcasted_iota(jnp.int32, (32, TOK), 0)
    number = (lax.broadcasted_iota(jnp.int32, (TOK, 1), 0) + 1 + core * TOK).astype(F32)
    weight = wts[...].T
    for o in range(3):
        one, two, three = WAYS[o]
        spot = ((coords[three] * 2 + (e & 1)) * 2 + core) * main_slots + sl
        if over:
            shared = 8 * main + (coords[three] * 2 + core) * over_slots + sl - main_slots
            spot = jnp.where(sl < main_slots, spot, shared)
        spot = jnp.where(sl >= 0, spot, -1).astype(F32).T
        line = coords[one] * 8 + coords[two]
        total = jnp.zeros((32, LANES), F32)
        for k in range(FAN):
            hit = lane == spot[:, k:k + 1]
            here = level == line[k:k + 1]
            there = level == line[k:k + 1] + 4
            for mask, value in ((here, number), (there, weight[:, k:k + 1])):
                total += jnp.dot(
                    mask.astype(F32).astype(BF16), jnp.where(hit, value, 0.0).astype(BF16), preferred_element_type=F32
                )
        tab[o] = total.reshape(4, 8, LANES)

    if over:
        number_e = lax.broadcasted_iota(jnp.int32, (2, 64, TOK), 1) * 2 + lax.broadcasted_iota(jnp.int32, (2, 64, TOK), 0)
        seen = jnp.zeros((2, 64, TOK), F32)
        for k in range(FAN):
            past = (sl[k:k + 1] >= main_slots)[None]
            seen = jnp.where((number_e == e[k:k + 1][None]) & past, 1.0, seen)
        seen = jnp.max(seen, axis=2, keepdims=True)
        flag[...] = jnp.broadcast_to(jnp.max(seen[0] * seen[1], axis=0, keepdims=True), flag.shape)

    def first_table(o, step, cc):
        one, _, _ = WAYS[o]
        return remote(
            tab.at[o, (place[one] + step) % 4], tab1.at[o, place[one], core],
            t1s.at[o, step, cc], t1r.at[o, step, cc], moved(place, one, step), (core + cc) % 2,
        )

    for o in range(3):
        one, _, _ = WAYS[o]
        for step in (1, 3, 2, 0):
            for cc in range(2):
                if step or cc:
                    first_table(o, step, cc).start()
        tab1[o, place[one], core] = tab[o, place[one]]

    def second(o, step, back):
        one, two, _ = WAYS[o]
        piece = gs[o].at[place[two], (place[one] + 4 - back) % 4]
        return remote(piece, piece, s2s.at[o, step, back], s2r.at[o, step, back], moved(place, two, step), core)

    def forward(o, up, back):
        one, two, _ = WAYS[o]
        piece = gs[o].at[(place[two] + (3 if up else 1)) % 4, (place[one] + 4 - back) % 4, 0 if up else 1]
        at = 0 if up else 2
        return remote(piece, piece, s2s.at[o, at, back], s2r.at[o, at, back], moved(place, two, 1 if up else 3), core)

    def second_wait(o, step, back):
        one, two, _ = WAYS[o]
        came = gs[o].at[(place[two] + 4 - step) % 4, (place[one] + 4 - back) % 4]
        remote(came, came, s2s.at[o, step, back], s2r.at[o, step, back], place, core).wait_recv()

    def forward_wait(o, up, back):
        one, two, _ = WAYS[o]
        at = 0 if up else 2
        came = gs[o].at[(place[two] + 2) % 4, (place[one] + 4 - back) % 4, 0 if up else 1]
        remote(came, came, s2s.at[o, at, back], s2r.at[o, at, back], place, core).wait_recv()

    def second_table(o, step):
        two = WAYS[o][1]
        return remote(
            tab2s.at[o, (place[two] + step) % 4], tab2.at[o, place[two]],
            t2s.at[o, step], t2r.at[o, step], moved(place, two, step), core,
        )

    def first_wait(o, step, cc):
        one, two, _ = WAYS[o]
        came = gs[o].at[place[two], (place[one] + 4 - step) % 4, (core + cc) % 2]
        remote(came, came, s1s.at[o, step, cc], s1r.at[o, step, cc], place, core).wait_recv()

    def first_table_wait(o, step, cc):
        one, _, _ = WAYS[o]
        came = tab1.at[o, (place[one] + 4 - step) % 4, (core + cc) % 2]
        remote(came, came, t1s.at[o, step, cc], t1r.at[o, step, cc], place, core).wait_recv()

    for back in (0, 1, 3, 2):
        for o in range(3):
            for cc in range(2):
                if back or cc:
                    first_wait(o, back, cc)
            for step in (1, 3):
                second(o, step, back).start()
    for o in range(3):
        for step in (0, 1, 3, 2):
            for cc in range(2):
                if step or cc:
                    first_table_wait(o, step, cc)
        for line in range(4):
            for a in range(4):
                tab2s[o, line, a:a + 1] = tab1[o, a, 0, line:line + 1] + tab1[o, a, 1, line:line + 1]
                tab2s[o, line, 4 + a:5 + a] = tab1[o, a, 0, 4 + line:5 + line] + tab1[o, a, 1, 4 + line:5 + line]
        for step in (1, 3, 2):
            second_table(o, step).start()
        two = WAYS[o][1]
        tab2[o, place[two]] = tab2s[o, place[two]]

    def landing(o, frm, group, to):
        if o == 0:
            return lambda h: to[0].at[h, frm, group]
        if o == 1:
            return lambda h: to[1].at[h, :, frm, group]
        return lambda h: to[2].at[h, group, :, frm]

    def third(o, step, cc, n, group):
        three = WAYS[o][2]
        to = (place[three] + step) % 4
        c = (core + cc) % 2
        src = rs[o].at[to * 2 + c, group]
        dst = landing(o, place[three], group, xs)(core)
        if step == 0 and cc == 0:
            return pltpu.make_async_copy(src, dst, s3r.at[o, 0, 0, n])
        return remote(src, dst, s3s.at[o, step, cc, n], s3r.at[o, step, cc, n], moved(place, three, step), c)

    def third_over(o, step, n, group):
        three = WAYS[o][2]
        src = ro[o].at[(place[three] + step) % 4, group]
        dst = landing(o, place[three], group, xo)(core)
        if step == 0:
            return pltpu.make_async_copy(src, dst, s3or.at[o, 0, n])
        return remote(src, dst, s3os.at[o, step, n], s3or.at[o, step, n], moved(place, three, step), core)

    def across(o, step, n, group, h):
        came = landing(o, (place[WAYS[o][2]] + 4 - step) % 4, group, xo)(h)
        return remote(came, came, fos.at[o, step, n], fors.at[o, step, n], place, 1 - core)

    def group_of(o, n):
        two = WAYS[o][1]
        gap = n ^ (n >> 1)
        return gap, (place[two] + 4 - gap) % 4

    token_lane = lax.broadcasted_iota(jnp.int32, (ROWS, 2 * TOK), 1).astype(F32) + 1.0

    def pack(o, n):
        three = WAYS[o][2]
        gap, group = group_of(o, n)
        column = tab2[o, group].T
        for a in range(4):
            pick = jnp.where(column[:ROWS, a:a + 1] == token_lane, 1.0, 0.0).astype(BF16)
            rows = jnp.dot(pick, gs[o][group, a].reshape(2 * TOK, WIDTH[o]), preferred_element_type=F32)
            rows = rows.astype(BF16)
            rs[o][:, group, a] = rows[:8 * main].reshape(8, main, WIDTH[o])
            if over:
                ro[o][:, group, a] = rows[8 * main:].reshape(4, over, WIDTH[o])
        for step in (1, 3, 2, 0):
            if over:
                third_over(o, step, n, group).start()
            for cc in range(2):
                third(o, step, cc, n, group).start()

    for o in range(3):
        pack(o, 0)
    for back in (0, 1, 3, 2):
        for o in range(3):
            for step in (1, 3):
                second_wait(o, step, back)
                forward(o, step == 1, back).start()

    def others(n, _):
        for o in range(3):
            gap, group = group_of(o, n)

            @pl.when(n == 3)
            def _():
                for back in range(4):
                    forward_wait(o, True, back)
                    forward_wait(o, False, back)

            came = tab2.at[o, group]
            remote(came, came, t2s.at[o, gap], t2r.at[o, gap], place, core).wait_recv()
            pack(o, n)
        return 0

    lax.fori_loop(1, 4, others, 0)

    for o in range(3):
        for step in range(4):
            for cc in range(2):
                if step or cc:
                    first(o, step, cc).wait_send()
                    first_table(o, step, cc).wait_send()
            if step:
                second_table(o, step).wait_send()
        for back in range(4):
            for step in (1, 3):
                second(o, step, back).wait_send()
                forward(o, step == 1, back).wait_send()

    for cp in loads:
        cp.wait()

    def shared_arrive(n, _):
        for o in range(3):
            gap, group = group_of(o, n)
            for step in range(4):
                if step == 0:
                    third_over(o, 0, n, group).wait()
                else:
                    came = landing(o, (place[WAYS[o][2]] + 4 - step) % 4, group, xo)(core)
                    remote(came, came, s3os.at[o, step, n], s3or.at[o, step, n], place, core).wait_recv()
                    third_over(o, step, n, group).wait_send()
                across(o, step, n, group, core).start()
        return 0

    def arrive(n, _):
        for o in range(3):
            three = WAYS[o][2]
            gap, group = group_of(o, n)
            for step in range(4):
                for cc in range(2):
                    came = landing(o, (place[three] + 4 - step) % 4, group, xs)((core + cc) % 2)
                    if step == 0 and cc == 0:
                        third(o, 0, 0, n, group).wait()
                    else:
                        remote(came, came, s3s.at[o, step, cc, n], s3r.at[o, step, cc, n], place, core).wait_recv()
                        third(o, step, cc, n, group).wait_send()
                if over:
                    across(o, step, n, group, core).wait_send()
                    across(o, step, n, group, 1 - core).wait_recv()
        return 0

    if over:
        lax.fori_loop(0, 4, shared_arrive, 0)
    lax.fori_loop(0, 4, arrive, 0)

    for o in range(3):
        for step in range(4):
            for cc in range(2):
                if step or cc:
                    pl.semaphore_signal(
                        free, inc=1, device_id=device(moved(place, WAYS[o][2], step), (core + cc) % 2), device_id_type=MESH
                    )

    mx, my, mz = place

    def send_a(s, x, q, cc, local):
        h = (core + cc) % 2
        src = xs[0].at[h, x, pl.ds(2 * q, 2)]
        dst = rs[0].at[mx * 2 + core, pl.ds(2 * q, 2)]
        if local:
            return pltpu.make_async_copy(src, dst, rar.at[s, cc])
        return remote(src, dst, ras.at[s, cc], rar.at[s, cc], (x, my, mz), h)

    def send_b(s, x, q, i, cc, local):
        h = (core + cc) % 2
        y = 2 * q + (my + i) % 2
        src = xs[1].at[h, x, y]
        dst = rs[1].at[my * 2 + core, :, x]
        if local:
            return pltpu.make_async_copy(src, dst, rbr.at[s, i, cc])
        return remote(src, dst, rbs.at[s, i, cc], rbr.at[s, i, cc], (mx, y, mz), h)

    def send_c(s, x, q, step, cc):
        h = (core + cc) % 2
        z = (mz + step) % 4
        src = xs[2].at[h, x, pl.ds(2 * q, 2), z]
        dst = rs[2].at[mz * 2 + core, x, pl.ds(2 * q, 2)]
        if step == 0 and cc == 0:
            return pltpu.make_async_copy(src, dst, rcr.at[s, 0, 0])
        return remote(src, dst, rcs.at[s, step, cc], rcr.at[s, step, cc], (mx, my, z), h)

    def over_a(s, x, q, local):
        src, dst = xo[0].at[core, x, pl.ds(2 * q, 2)], ro[0].at[mx, pl.ds(2 * q, 2)]
        if local:
            return pltpu.make_async_copy(src, dst, oar.at[s])
        return remote(src, dst, oas.at[s], oar.at[s], (x, my, mz), core)

    def over_b(s, x, q, i, local):
        y = 2 * q + (my + i) % 2
        src, dst = xo[1].at[core, x, y], ro[1].at[my, :, x]
        if local:
            return pltpu.make_async_copy(src, dst, obr.at[s, i])
        return remote(src, dst, obs.at[s, i], obr.at[s, i], (mx, y, mz), core)

    def over_c(s, x, q, step):
        z = (mz + step) % 4
        src, dst = xo[2].at[core, x, pl.ds(2 * q, 2), z], ro[2].at[mz, x, pl.ds(2 * q, 2)]
        if step == 0:
            return pltpu.make_async_copy(src, dst, ocr.at[s, 0])
        return remote(src, dst, ocs.at[s, step], ocr.at[s, step], (mx, my, z), core)

    def each_over(s, o, act):
        x, q = block_of(s)
        if o == 0:
            @pl.when(s % 4 < 3)
            def _():
                act(over_a(s, x, q, False))

            @pl.when(s % 4 == 3)
            def _():
                act(over_a(s, x, q, True))
        elif o == 1:
            act(over_b(s, x, q, 1, False))

            @pl.when(s < 4)
            def _():
                act(over_b(s, x, q, 0, False))

            @pl.when(s >= 4)
            def _():
                act(over_b(s, x, q, 0, True))
        else:
            for step in (1, 3, 2, 0):
                act(over_c(s, x, q, step))

    def to_sibling(s, o):
        x, q = block_of(s)
        return remote(
            xo[o].at[1 - core, x, pl.ds(2 * q, 2)], ys[o].at[x, pl.ds(2 * q, 2)],
            yss.at[s, o], ysr.at[s, o], place, 1 - core,
        )

    def merge(s):
        x, q = block_of(s)
        pair = pl.ds(2 * q, 2)
        for o in range(3):
            to_sibling(s, o).wait_recv()
            mine = xo[o][core, x, pair].reshape(8 * over, WIDTH[o]).astype(F32)
            theirs = ys[o][x, pair].reshape(8 * over, WIDTH[o]).astype(F32)
            kept = jnp.where(hot > 0.0, mine, theirs).astype(BF16)
            xo[o][core, x, pair] = kept.reshape(2, 4, over, WIDTH[o])
            each_over(s, o, lambda cp: cp.start())

    if over:
        me = ((mz * 4 + my) * 4 + mx) * 2 + core
        filled = jnp.where((ids[...] == me) & (slots[...] >= main_slots), 1.0, 0.0)
        hot = jnp.max(jnp.max(filled, axis=1, keepdims=True), axis=0, keepdims=True)

    def block_of(s):
        turn = (s + 1) % 4
        return (mx + (turn ^ (turn >> 1))) % 4, (my // 2 + 1 - s // 4) % 2

    def each(s, o, act):
        x, q = block_of(s)
        for cc in range(2):
            if o == 0 and cc:
                act(send_a(s, x, q, cc, False))
            elif o == 0:
                @pl.when(s % 4 < 3)
                def _():
                    act(send_a(s, x, q, 0, False))

                @pl.when(s % 4 == 3)
                def _():
                    act(send_a(s, x, q, 0, True))
            elif o == 1:
                for i in range(2):
                    if cc or i:
                        act(send_b(s, x, q, i, cc, False))
                    else:
                        @pl.when(s < 4)
                        def _():
                            act(send_b(s, x, q, 0, 0, False))

                        @pl.when(s >= 4)
                        def _():
                            act(send_b(s, x, q, 0, 0, True))
            else:
                for step in (1, 3, 2, 0):
                    act(send_c(s, x, q, step, cc))

    def expert(s, _):
        x, q = block_of(s)
        pair = pl.ds(2 * q, 2)
        halves = [(h, o) for h in range(2) for o in range(3)]
        rows = jnp.concatenate([xs[o][h, x, pair].reshape(8 * main, WIDTH[o]) for h, o in halves], axis=1)
        if over:
            shared = jnp.concatenate([xo[o][h, x, pair].reshape(8 * over, WIDTH[o]) for h, o in halves], axis=1)
            rows = jnp.concatenate([rows, shared], axis=0)
        for f in range(0, FF, 256):
            gate = jnp.dot(rows, wg[:, f:f + 256], preferred_element_type=F32)
            up = jnp.dot(rows, wu[:, f:f + 256], preferred_element_type=F32)
            hidden[:, f:f + 256] = (gate / (1.0 + jnp.exp(-gate)) * up).astype(BF16)
        for h in range(2):
            for o in range(3):
                lo = h * HALF + START[o]
                res = jnp.dot(hidden[...], wd[:, lo:lo + WIDTH[o]], preferred_element_type=F32)
                res = res.astype(BF16)
                xs[o][h, x, pair] = res[:8 * main].reshape(2, 4, main, WIDTH[o])
                if over:
                    xo[o][h, x, pair] = res[8 * main:].reshape(2, 4, over, WIDTH[o])

        @pl.when(s == 0)
        def _():
            pl.semaphore_wait(free, 21)

        for o in range(3):
            if over:
                to_sibling(s, o).start()
            each(s, o, lambda cp: cp.start())
        if over:
            @pl.when(s > 0)
            def _():
                merge(s - 1)
        return 0

    lax.fori_loop(0, 8, expert, 0)
    if over:
        merge(7)

    def returned(o):
        def one_block(s, _):
            each(s, o, lambda cp: cp.wait())
            if over:
                each_over(s, o, lambda cp: cp.wait())
                to_sibling(s, o).wait_send()
            return 0

        lax.fori_loop(0, 8, one_block, 0)

    token_row = lax.broadcasted_iota(jnp.int32, (2 * TOK, ROWS), 0).astype(F32) + 1.0

    FAR, DIRECT, SUM = range(3)

    def push(o, up, kind, turn):
        one, two, _ = WAYS[o]
        step, c = (1, 0) if up else (3, 1)
        a = (place[one] + turn) % 4
        group = (place[two] + (2 if kind == FAR else step)) % 4
        if kind == DIRECT:
            c = 1 - c
        slot = 2 if kind == FAR else step // 2
        at = kind if up else 3 + kind
        return remote(
            gs[o].at[group, a, c], acc2[o].at[slot, a, c],
            q2s.at[o, at, turn], q2r.at[o, at, turn], moved(place, two, step), core,
        )

    def combine(o, step):
        one, two, _ = WAYS[o]
        group = (place[two] + step) % 4
        for turn in (1, 3, 2, 0):
            a = (place[one] + turn) % 4
            index = tab2[o, group, pl.ds(a, 1), :ROWS]
            w = tab2[o, group, pl.ds(4 + a, 1), :ROWS]
            mix = jnp.where(index == token_row, w, 0.0).astype(BF16)
            rows = rs[o][:, group, a].reshape(8 * main, WIDTH[o])
            if over:
                rows = jnp.concatenate([rows, ro[o][:, group, a].reshape(4 * over, WIDTH[o])], axis=0)
            part = jnp.dot(mix, rows, preferred_element_type=F32)
            gs[o][group, a] = part.astype(BF16).reshape(2, TOK, WIDTH[o])
            if step == 2:
                push(o, True, FAR, turn).start()
                push(o, False, FAR, turn).start()
            elif step:
                push(o, step == 1, DIRECT, turn).start()

    returned(2)
    for step in (2, 1, 3, 0):
        combine(2, step)
    returned(0)
    returned(1)
    for step in (2, 1, 3, 0):
        combine(0, step)
        combine(1, step)

    for turn in (1, 3, 2, 0):
        for o in (2, 0, 1):
            one, two, _ = WAYS[o]
            a = (place[one] + turn) % 4
            for up in (True, False):
                step, c = (1, 0) if up else (3, 1)
                group = (place[two] + step) % 4
                push(o, up, FAR, turn).wait_recv()
                gs[o][group, a, c] = (gs[o][group, a, c].astype(F32) + acc2[o][2, a, c].astype(F32)).astype(BF16)
                push(o, up, SUM, turn).start()

    def reduce_first(o, step, cc):
        one, two, _ = WAYS[o]
        c = (core + cc) % 2
        return remote(
            gs[o].at[place[two], (place[one] + step) % 4, c], acc1[o].at[step, cc],
            q1s.at[o, step, cc], q1r.at[o, step, cc], moved(place, one, step), c,
        )

    for step in (1, 3, 2, 0):
        for o in (2, 0, 1):
            one, two, _ = WAYS[o]
            a = (place[one] + step) % 4
            for up in (True, False):
                push(o, up, FAR, step).wait_send()
                push(o, up, DIRECT, step).wait()
                push(o, up, SUM, step).wait()
            total = gs[o][place[two], a].astype(F32)
            for n in range(2):
                total += acc2[o][n, a].astype(F32)
            gs[o][place[two], a] = total.astype(BF16)
            for cc in range(2):
                if step or cc:
                    reduce_first(o, step, cc).start()
            if step == 0:
                acc1[o][0, 0] = gs[o][place[two], place[one], core]

    for o in (2, 0, 1):
        for step in range(4):
            for cc in range(2):
                if step or cc:
                    reduce_first(o, step, cc).wait()
        for cc in range(2):
            h = (core + cc) % 2
            where = pl.ds(pl.multiple_of(h * HALF + START[o], 128), WIDTH[o])
            total = acc1[o][0, cc].astype(F32)
            for step in (1, 2, 3):
                total += acc1[o][step, cc].astype(F32)
            out[:, where] = (resid[:, where].astype(F32) + total).astype(BF16)


def layer(main, over, number, resid, gain, ids, slots, wts, w_gate, w_up, w_down):
    vmem = pl.BlockSpec(memory_space=pltpu.VMEM)
    hbm = pl.BlockSpec(memory_space=pl.ANY)
    lanes = -(-(8 * main + 4 * over) // 128) * 128

    def per_way(*lead, rows):
        return [pltpu.VMEM((*lead, rows, w), BF16) for w in WIDTH]

    def pairs(*shapes):
        return [pltpu.SemaphoreType.DMA(shape) for shape in shapes for _ in range(2)]

    scratch = [
        *per_way(2, rows=TOK),
        *per_way(4, 4, 2, rows=TOK),
        *per_way(8, 4, 4, rows=main),
        *per_way(2, 4, 4, 4, rows=main),
        *per_way(3, 4, 2, rows=TOK),
        *per_way(4, 2, rows=TOK),
        pltpu.VMEM((3, 4, 8, lanes), F32),
        pltpu.VMEM((3, 4, 2, 8, lanes), F32),
        pltpu.VMEM((3, 4, 8, lanes), F32),
        pltpu.VMEM((3, 4, 8, lanes), F32),
        pltpu.VMEM((8 * (main + over), FF), BF16),
        pltpu.VMEM((D, FF), BF16),
        pltpu.VMEM((D, FF), BF16),
        pltpu.VMEM((FF, D), BF16),
        pltpu.SemaphoreType.DMA((3,)),
        *pairs((3, 4, 2), (3, 4, 2), (3, 4, 4), (3, 4), (3, 4, 2, 4), (8, 2), (8, 2, 2), (8, 4, 2), (3, 6, 4), (3, 4, 2)),
        pltpu.SemaphoreType.REGULAR,
    ]
    if over:
        scratch += [
            *per_way(4, 4, 4, rows=over),
            *per_way(2, 4, 4, 4, rows=over),
            *per_way(4, 4, 4, rows=over),
            *pairs((3, 4, 4), (3, 4, 4), (8,), (8, 2), (8, 4), (8, 3)),
        ]
    return pl.pallas_call(
        functools.partial(kernel, main, over),
        out_shape=(jax.ShapeDtypeStruct((TOK, D), BF16), jax.ShapeDtypeStruct((8, 128), F32)) if over
        else jax.ShapeDtypeStruct((TOK, D), BF16),
        in_specs=[vmem] * 5 + [hbm] * 3,
        out_specs=(vmem, vmem) if over else vmem,
        scratch_shapes=scratch,
        compiler_params=pltpu.CompilerParams(
            collective_id=number, has_side_effects=True, vmem_limit_bytes=62 * 2**20
        ),
        cost_estimate=pl.CostEstimate(flops=30 * 10**9, bytes_accessed=11 * 10**6, transcendentals=2 * 10**6),
    )(resid, gain, ids, slots, wts, w_gate, w_up, w_down)


def per_device(resid, norm_gain, w_gate, w_up, w_down, route_ids, route_slots, route_weights):
    args = (
        resid, norm_gain[None, :], route_ids.T, route_slots.T, route_weights.T, w_gate[0], w_up[0], w_down[0],
    )
    result, flag = layer(MAIN, OVER, 0, *args)
    return lax.cond(flag[0, 0] > 0.5, lambda result, *args: layer(2 * CAP, 0, 1, *args), lambda result, *args: result, result, *args)


def solution(mesh):
    rows = P(("dp", "expert"), None)
    expert = P(("dp", "expert"), None, None)
    return jax.shard_map(
        per_device, mesh=mesh, in_specs=(rows, P(), expert, expert, expert, rows, rows, rows), out_specs=rows, check_vma=False
    )
```

profile of v0, /device:TPU:3, one launch (start us, length us, event | category | flops | bytes accessed | tf_op | source)
XLA Modules:
  0.0 170.9 jit_solution(5742862754530957299)
XLA Ops:
  0.0 0.0 copy-start
  0.0 0.0 copy-start.1
  0.0 0.0 copy-start.2
  0.0 0.0 copy-start.3
  0.0 0.0 copy-start.4
  0.0 167.9 %shard_map.84 = (bf16[128,2048]{1,0:T(8,128)(2,1)S(1)}, f32[8,128]{1,0:T(8,128)}) custom-call(bf16[128,2048]{1,0:T(8,128)(2,1)} %resid.1, f32[1,2048]{1,0:T(1,128)} %bitcast.14, s32[8,128]{1,0:T(8,128)} %bitcast.16, s32[8,128]{1,0:T(8,128)} %bitcast.18, f32[8,128]{1,0:T(8,128)} %bitcast.20, bf16[2048,768]{1,0:T(8,128)(2,1)} %bitcast.8, ...), custom_call_target="tpu_custom_call" | custom-call | flops 30000001024 | bytes 11000000 | tf_op jit(solution)/shard_map/pallas_call | solution.py:665
  168.0 1.2 slice.3
  169.8 0.0 copy-done
  169.8 0.0 copy-done.1
  169.8 0.0 copy-done.2
  169.8 0.0 copy-done.3
  169.8 0.0 copy-done.4
  169.8 0.3 conditional.1
  170.1 0.8 copy.14
Async XLA Ops:
  0.0 169.8 %copy-start = (bf16[128,2048]{1,0:T(8,128)(2,1)S(1)}, bf16[128,2048]{1,0:T(8,128)(2,1)}, u32[]{:S(2)}) copy-start(bf16[128,2048]{1,0:T(8,128)(2,1)} %resid.1) | copy-start | bytes 1572868
  0.0 169.8 %copy-start.1 = (f32[2048]{0:T(1024)S(1)}, f32[2048]{0:T(1024)}, u32[]{:S(2)}) copy-start(f32[2048]{0:T(1024)} %param.11) | copy-start | bytes 24580
  0.0 169.8 %copy-start.2 = (s32[128,8]{0,1:T(8,128)S(1)}, s32[128,8]{0,1:T(8,128)}, u32[]{:S(2)}) copy-start(s32[128,8]{0,1:T(8,128)} %param.15) | copy-start | bytes 12292
  0.0 169.8 %copy-start.3 = (s32[128,8]{0,1:T(8,128)S(1)}, s32[128,8]{0,1:T(8,128)}, u32[]{:S(2)}) copy-start(s32[128,8]{0,1:T(8,128)} %param.16) | copy-start | bytes 12292
  0.0 169.8 %copy-start.4 = (f32[128,8]{0,1:T(8,128)S(1)}, f32[128,8]{0,1:T(8,128)}, u32[]{:S(2)}) copy-start(f32[128,8]{0,1:T(8,128)} %param.17) | copy-start | bytes 12292
where the time goes:
time: 171 us
  Pallas kernels  168 us (98%)
  local copies, waits for them, and re-layouts  2 us (1%)
    pallas_call x1, Pallas kernels, layer(): pl.pallas_call(functools.partial(kernel, main, over), out_shape=(jax.Shap...  168 us

commit v1 on v0

--- a/solution.py
+++ b/solution.py
@@ -518,7 +518,7 @@
     if over:
         merge(7)
 
-    def returned(o):
+    def returned(o, begin=0, end=8):
         def one_block(s, _):
             each(s, o, lambda cp: cp.wait())
             if over:
@@ -526,7 +526,7 @@
                 to_sibling(s, o).wait_send()
             return 0
 
-        lax.fori_loop(0, 8, one_block, 0)
+        lax.fori_loop(begin, end, one_block, 0)
 
     token_row = lax.broadcasted_iota(jnp.int32, (2 * TOK, ROWS), 0).astype(F32) + 1.0
 
@@ -565,12 +565,15 @@
             elif step:
                 push(o, step == 1, DIRECT, turn).start()
 
+    returned(0, 0, 4)
+    combine(0, 2)
     returned(2)
     for step in (2, 1, 3, 0):
         combine(2, step)
-    returned(0)
+    returned(0, 4, 8)
     returned(1)
-    for step in (2, 1, 3, 0):
+    combine(1, 2)
+    for step in (1, 3, 0):
         combine(0, step)
         combine(1, step)
 

time: 171 us -> 170 us (level)
  no operation moved by 1% of the time
where the time goes in v1:
time: 170 us
  Pallas kernels  167 us (98%)
  local copies, waits for them, and re-layouts  2 us (1%)
    pallas_call x1, Pallas kernels, layer(): pl.pallas_call(functools.partial(kernel, main, over), out_shape=(jax.Shap...  167 us

profile of v1, /device:TPU:3, one launch (start us, length us, event | category | flops | bytes accessed | tf_op | source)
XLA Modules:
  0.0 170.0 jit_solution(16050354753033582163)
XLA Ops:
  0.0 0.0 copy-start
  0.0 0.0 copy-start.1
  0.0 0.0 copy-start.2
  0.0 0.0 copy-start.3
  0.0 0.0 copy-start.4
  0.0 167.0 %shard_map.84 = (bf16[128,2048]{1,0:T(8,128)(2,1)S(1)}, f32[8,128]{1,0:T(8,128)}) custom-call(bf16[128,2048]{1,0:T(8,128)(2,1)} %resid.1, f32[1,2048]{1,0:T(1,128)} %bitcast.14, s32[8,128]{1,0:T(8,128)} %bitcast.16, s32[8,128]{1,0:T(8,128)} %bitcast.18, f32[8,128]{1,0:T(8,128)} %bitcast.20, bf16[2048,768]{1,0:T(8,128)(2,1)} %bitcast.8, ...), custom_call_target="tpu_custom_call" | custom-call | flops 30000001024 | bytes 11000000 | tf_op jit(solution)/shard_map/pallas_call | solution.py:668
  167.1 1.2 slice.3
  168.9 0.0 copy-done
  168.9 0.0 copy-done.1
  168.9 0.0 copy-done.2
  168.9 0.0 copy-done.3
  169.0 0.0 copy-done.4
  169.0 0.3 conditional.1
  169.2 0.8 copy.14
Async XLA Ops:
  0.0 168.9 %copy-start = (bf16[128,2048]{1,0:T(8,128)(2,1)S(1)}, bf16[128,2048]{1,0:T(8,128)(2,1)}, u32[]{:S(2)}) copy-start(bf16[128,2048]{1,0:T(8,128)(2,1)} %resid.1) | copy-start | bytes 1572868
  0.0 168.9 %copy-start.1 = (f32[2048]{0:T(1024)S(1)}, f32[2048]{0:T(1024)}, u32[]{:S(2)}) copy-start(f32[2048]{0:T(1024)} %param.11) | copy-start | bytes 24580
  0.0 168.9 %copy-start.2 = (s32[128,8]{0,1:T(8,128)S(1)}, s32[128,8]{0,1:T(8,128)}, u32[]{:S(2)}) copy-start(s32[128,8]{0,1:T(8,128)} %param.15) | copy-start | bytes 12292
  0.0 168.9 %copy-start.3 = (s32[128,8]{0,1:T(8,128)S(1)}, s32[128,8]{0,1:T(8,128)}, u32[]{:S(2)}) copy-start(s32[128,8]{0,1:T(8,128)} %param.16) | copy-start | bytes 12292
  0.0 168.9 %copy-start.4 = (f32[128,8]{0,1:T(8,128)S(1)}, f32[128,8]{0,1:T(8,128)}, u32[]{:S(2)}) copy-start(f32[128,8]{0,1:T(8,128)} %param.17) | copy-start | bytes 12292

commit v2 on v1

--- a/solution.py
+++ b/solution.py
@@ -568,12 +568,12 @@
     returned(0, 0, 4)
     combine(0, 2)
     returned(2)
-    for step in (2, 1, 3, 0):
+    for step in (2, 1, 3):
         combine(2, step)
     returned(0, 4, 8)
     returned(1)
     combine(1, 2)
-    for step in (1, 3, 0):
+    for step in (1, 3):
         combine(0, step)
         combine(1, step)
 
@@ -587,6 +587,9 @@
                 push(o, up, FAR, turn).wait_recv()
                 gs[o][group, a, c] = (gs[o][group, a, c].astype(F32) + acc2[o][2, a, c].astype(F32)).astype(BF16)
                 push(o, up, SUM, turn).start()
+
+    for o in (2, 0, 1):
+        combine(o, 0)
 
     def reduce_first(o, step, cc):
         one, two, _ = WAYS[o]

time: 170 us -> 170 us (level)
  no operation moved by 1% of the time
where the time goes in v2:
time: 170 us
  Pallas kernels  167 us (98%)
  local copies, waits for them, and re-layouts  2 us (1%)
    pallas_call x1, Pallas kernels, layer(): pl.pallas_call(functools.partial(kernel, main, over), out_shape=(jax.Shap...  167 us

profile of v2, /device:TPU:3, one launch (start us, length us, event | category | flops | bytes accessed | tf_op | source)
XLA Modules:
  0.0 170.0 jit_solution(14893125345516896591)
XLA Ops:
  0.0 0.0 copy-start
  0.0 0.0 copy-start.1
  0.0 0.0 copy-start.2
  0.0 0.0 copy-start.3
  0.0 0.0 copy-start.4
  0.0 167.0 %shard_map.84 = (bf16[128,2048]{1,0:T(8,128)(2,1)S(1)}, f32[8,128]{1,0:T(8,128)}) custom-call(bf16[128,2048]{1,0:T(8,128)(2,1)} %resid.1, f32[1,2048]{1,0:T(1,128)} %bitcast.14, s32[8,128]{1,0:T(8,128)} %bitcast.16, s32[8,128]{1,0:T(8,128)} %bitcast.18, f32[8,128]{1,0:T(8,128)} %bitcast.20, bf16[2048,768]{1,0:T(8,128)(2,1)} %bitcast.8, ...), custom_call_target="tpu_custom_call" | custom-call | flops 30000001024 | bytes 11000000 | tf_op jit(solution)/shard_map/pallas_call | solution.py:671
  167.1 1.2 slice.3
  168.9 0.0 copy-done
  168.9 0.0 copy-done.1
  168.9 0.0 copy-done.2
  168.9 0.0 copy-done.3
  168.9 0.0 copy-done.4
  169.0 0.3 conditional.1
  169.2 0.8 copy.14
Async XLA Ops:
  0.0 168.9 %copy-start = (bf16[128,2048]{1,0:T(8,128)(2,1)S(1)}, bf16[128,2048]{1,0:T(8,128)(2,1)}, u32[]{:S(2)}) copy-start(bf16[128,2048]{1,0:T(8,128)(2,1)} %resid.1) | copy-start | bytes 1572868
  0.0 168.9 %copy-start.1 = (f32[2048]{0:T(1024)S(1)}, f32[2048]{0:T(1024)}, u32[]{:S(2)}) copy-start(f32[2048]{0:T(1024)} %param.11) | copy-start | bytes 24580
  0.0 168.9 %copy-start.2 = (s32[128,8]{0,1:T(8,128)S(1)}, s32[128,8]{0,1:T(8,128)}, u32[]{:S(2)}) copy-start(s32[128,8]{0,1:T(8,128)} %param.15) | copy-start | bytes 12292
  0.0 168.9 %copy-start.3 = (s32[128,8]{0,1:T(8,128)S(1)}, s32[128,8]{0,1:T(8,128)}, u32[]{:S(2)}) copy-start(s32[128,8]{0,1:T(8,128)} %param.16) | copy-start | bytes 12292
  0.0 168.9 %copy-start.4 = (f32[128,8]{0,1:T(8,128)S(1)}, f32[128,8]{0,1:T(8,128)}, u32[]{:S(2)}) copy-start(f32[128,8]{0,1:T(8,128)} %param.17) | copy-start | bytes 12292
